TPU v7x, 512 devices: a whole 4x4x16 slice. The times are simulated.
512 devices in a mesh: dp: 4 (over y), ctx: 64 (over x, z), mp: 2 (over core).
Axes of the slice: x: 4, y: 4, z: 16, core: 2. Of those that a mesh axis runs over, the one named last changes fastest.
Arguments:
- features: bfloat16 [4, 8192, 3, 4096], P('dp', 'ctx', None, 'mp'), may hold values from -6 to 6
- conv_weight: float32 [7, 3, 4096], P(None, None, 'mp'), may hold values from -2 to 2
- log_rate: float32 [8, 32], P(None, 'mp'), as said below
- residues: float32 [8, 4096], P(None, 'mp'), may hold values from -4 to 4
- skip_weight: float32 [4096], P('mp'), may hold values from 0.5 to 1.5
- norm_gain: float32 [4096], P('mp'), may hold values from 0.5 to 1.5
- cotangent: bfloat16 [4, 8192, 4096], P('dp', 'ctx', 'mp'), may hold values from -6 to 6
Outputs:
- block_out: bfloat16 [4, 8192, 4096], P('dp', 'ctx', 'mp')
- feature_grad: bfloat16 [4, 8192, 3, 4096], P('dp', 'ctx', None, 'mp')
- conv_grad: float32 [7, 3, 4096], P(None, None, 'mp')
- rate_grad: float32 [8, 32], P(None, 'mp')
- residue_grad: float32 [8, 4096], P(None, 'mp')
- skip_grad: float32 [4096], P('mp')
- gain_grad: float32 [4096], P('mp')
Inputs may be any that keep to these rules, and one draw needn't show every extreme that they name: log_rate lies between ln(1 / 1048576) and ln(1 / 16).
All inputs are finite; a program needn't handle non-finite values.
Results may differ from a plain program's by a relative error of at most 0.0011.
Values may be sent and summed in bfloat16 or wider, within the bound.
No kernel may reach another device: no remote copies, remote signals or barrier semaphores. Data moves between devices by JAX's collectives and lax.ppermute only.
A program may use at most 128 MiB of HBM per device.

v0:
```python
import jax
import jax.numpy as jnp
from jax import lax
from jax.sharding import PartitionSpec as P

D = 4096
EPSILON = 1e-06
HIGHEST = lax.Precision.HIGHEST


def passed_along(value, axis, steps):
    count = lax.axis_size(axis)
    leading, last = (max(0, -steps), min(count, count - steps))
    return lax.ppermute(value, axis, [(source, source + steps) for source in range(leading, last)])


def carried_in(part, axis, combine, identity, reverse):
    count = lax.axis_size(axis)
    place = lax.axis_index(axis)
    ahead = count - 1 - place if reverse else place
    gathered = jax.tree.map(lambda a: lax.all_gather(a, axis), part)
    state = jax.tree.map(lambda a, e: jnp.zeros_like(a) + jnp.asarray(e, a.dtype), part, identity)

    def one(lap, state):
        source = count - 1 - lap if reverse else lap
        return combine(
            state, jax.tree.map(lambda a: lax.dynamic_index_in_dim(a, source, 0, False), gathered)
        )

    return lax.fori_loop(0, ahead, one, state)


def decay_matrix(rate_row, length):
    places = jnp.arange(length, dtype=jnp.float32)
    lagged = places[:, None] - places[None, :]
    clipped = jnp.maximum(lagged, 0.0)
    matrix = jnp.where(lagged >= 0, jnp.exp(-rate_row[:, None, None] * clipped), 0.0)
    return (matrix, clipped)


def compose_back(earlier, later):
    return (earlier[0] * later[0], earlier[1] * later[0][..., None] + later[1])


def local(features, conv_weight, log_rate, residues, skip_weight, norm_gain, cotangent):
    local_feats = features[0]
    length = local_feats.shape[0]
    channels = local_feats.shape[2]
    pole_count = log_rate.shape[0]
    groups_here = log_rate.shape[1]
    group_size = channels // groups_here
    halo_rows = conv_weight.shape[0] - 1
    previous = passed_along(local_feats[length - halo_rows :], "ctx", 1)
    extended = jnp.concatenate([previous, local_feats], axis=0)
    filtered = conv_weight[0] * extended[halo_rows : halo_rows + length]
    for offset in range(1, halo_rows + 1):
        filtered = (
            filtered
            + conv_weight[offset] * extended[halo_rows - offset : halo_rows - offset + length]
        )
    query_rows = filtered[:, 0]
    key_rows = filtered[:, 1]
    value_rows = filtered[:, 2]
    product = key_rows * value_rows
    rate_rows = jnp.exp(log_rate).T
    grouped = product.reshape(length, groups_here, group_size).transpose(1, 0, 2)
    places = jnp.arange(length, dtype=jnp.float32)
    tail_lag = length - 1.0 - places
    block_decay = jnp.exp(-rate_rows * length)

    def forward_plain(pieces):
        rate_row, product_block = pieces
        matrix, clipped = decay_matrix(rate_row, length)
        return jnp.einsum("pts,sc->ptc", matrix, product_block, precision=HIGHEST)

    local_states = lax.map(forward_plain, (rate_rows, grouped))
    end_rows = local_states[:, :, length - 1, :]
    carried = carried_in(
        (block_decay, end_rows),
        "ctx",
        compose_back,
        (jnp.ones_like(block_decay), jnp.zeros_like(end_rows)),
        False,
    )
    state_in = carried[1]
    head_decay = jnp.exp(-rate_rows[:, :, None] * (places + 1.0))
    states = local_states + head_decay[..., None] * state_in[:, :, None, :]
    weights = residues.reshape(pole_count, groups_here, group_size).transpose(1, 0, 2)
    modal_part = jnp.einsum("gptc,gpc->tgc", states, weights, precision=HIGHEST).reshape(
        length, channels
    )
    branch = modal_part + skip_weight * product
    gated_rows = query_rows * branch
    seed_grad = cotangent[0].astype(jnp.float32)
    scaled_grad = norm_gain * seed_grad
    square_sum = lax.psum(jnp.sum(gated_rows * gated_rows, axis=1), "mp")
    inv_rms = lax.rsqrt(square_sum / D + EPSILON)[:, None]
    normed = gated_rows * inv_rms
    block_out = (norm_gain * normed).astype(jnp.bfloat16)
    slope_sum = lax.psum(jnp.sum(scaled_grad * gated_rows, axis=1), "mp")
    gain_local = jnp.sum(seed_grad * normed, axis=0)
    dgated = scaled_grad * inv_rms - gated_rows * (
        slope_sum[:, None] * inv_rms * inv_rms * inv_rms / D
    )
    dquery = dgated * branch
    dbranch = dgated * query_rows
    skip_local = jnp.sum(dbranch * product, axis=0)
    dgrouped = dbranch.reshape(length, groups_here, group_size).transpose(1, 0, 2)
    back_in = jnp.einsum("gpt,gtc->gpc", head_decay, dgrouped, precision=HIGHEST)
    returned = carried_in(
        (block_decay, back_in),
        "ctx",
        compose_back,
        (jnp.ones_like(block_decay), jnp.zeros_like(back_in)),
        True,
    )
    later_in = returned[1]

    def backward_adjoint(pieces):
        (
            rate_row,
            product_block,
            grad_block,
            state_block,
            weight_row,
            later_row,
            start_row,
            slope_row,
        ) = pieces
        matrix, clipped = decay_matrix(rate_row, length)
        residue_part = jnp.sum(grad_block[None] * state_block, axis=1)
        tail_row = jnp.exp(-rate_row[:, None] * tail_lag)
        adjoint = (
            jnp.einsum("pts,tc->psc", matrix, grad_block, precision=HIGHEST)
            + tail_row[..., None] * later_row[:, None, :]
        )
        inner = (
            jnp.sum(adjoint[:, 1:, :] * state_block[:, : length - 1, :], axis=1)
            + adjoint[:, 0, :] * start_row
        )
        rate_part = -jnp.exp(-rate_row) * jnp.sum(weight_row * inner, axis=1)
        return (residue_part, rate_part, jnp.sum(weight_row[:, None, :] * adjoint, axis=0))

    residue_parts, rate_parts, dproduct_groups = lax.map(
        backward_adjoint,
        (rate_rows, grouped, dgrouped, states, weights, later_in, state_in, state_in),
    )
    residue_local = residue_parts.transpose(1, 0, 2).reshape(pole_count, channels)
    rate_local = rate_parts.T * jnp.exp(log_rate)
    dproduct = dproduct_groups.transpose(1, 0, 2).reshape(length, channels) + dbranch * skip_weight
    dfiltered = jnp.stack([dquery, dproduct * value_rows, dproduct * key_rows], axis=1)
    zeros_rim = jnp.zeros((halo_rows, 3, channels), jnp.float32)
    padded_grad = jnp.concatenate([zeros_rim, dfiltered, zeros_rim], axis=0)
    dextended = conv_weight[0] * padded_grad[0 : length + halo_rows]
    for offset in range(1, halo_rows + 1):
        dextended = (
            dextended + conv_weight[offset] * padded_grad[offset : offset + length + halo_rows]
        )
    conv_local = jnp.stack(
        [
            jnp.sum(dfiltered * extended[halo_rows - offset : halo_rows - offset + length], axis=0)
            for offset in range(halo_rows + 1)
        ],
        axis=0,
    )
    incoming = passed_along(dextended[:halo_rows], "ctx", -1)
    dlocal = dextended[halo_rows:] + jnp.concatenate(
        [jnp.zeros((length - halo_rows, 3, channels), jnp.float32), incoming], axis=0
    )
    feature_grad = dlocal.astype(jnp.bfloat16)[None]
    totals = lax.psum(
        (conv_local, rate_local, residue_local, skip_local, gain_local), ("dp", "ctx")
    )
    return (block_out[None], feature_grad, totals[0], totals[1], totals[2], totals[3], totals[4])


def solution(mesh):
    in_specs = (
        P("dp", "ctx", None, "mp"),
        P(None, None, "mp"),
        P(None, "mp"),
        P(None, "mp"),
        P("mp"),
        P("mp"),
        P("dp", "ctx", "mp"),
    )
    out_specs = (
        P("dp", "ctx", "mp"),
        P("dp", "ctx", None, "mp"),
        P(None, None, "mp"),
        P(None, "mp"),
        P(None, "mp"),
        P("mp"),
        P("mp"),
    )
    return jax.shard_map(local, mesh=mesh, in_specs=in_specs, out_specs=out_specs, check_vma=False)
```

profile of v0, /device:TPU:0, one launch (start us, length us, event | category | flops | bytes accessed | tf_op | source)
XLA Modules:
  0.0 2139.7 jit_solution(14530745588208930304)
XLA Ops:
  12.5 7.9 fusion.48
  25.0 38.0 %while.51 = (s32[]{:T(128)}, f32[16,8,128,128]{3,2,1,0:T(8,128)}, f32[16,8]{1,0:T(8,128)S(1)}, f32[16,128,128]{2,1,0:T(8,128)}, s32[]{:T(128)}) while((s32[]{:T(128)}, f32[16,8,128,128]{3,2,1,0:T(8,128)}, f32[16,8]{1,0:T(8,128)S(1)}, f32[16,128,128]{2,1,0:T(8,128)}, s32[]{:T(128)}) %tuple.143), condition=%wide.region_1.2_spmd, body=%wide.region_0.1_spmd.sunk | while | flops 201654288 | bytes 754849 | solution.py:76
  25.1 2.3 fusion.110
  27.5 2.3 fusion.110
  29.9 2.3 fusion.110
  34.6 2.3 fusion.110
  41.7 2.3 fusion.110
  44.1 2.3 fusion.110
  46.5 2.3 fusion.110
  48.9 2.3 fusion.110
  58.3 2.3 fusion.110
  60.7 2.3 fusion.110
  63.0 9.9 copy.50
  76.2 91.5 %all-gather.3 = f32[64,16,8]{1,2,0:T(8,128)} all-gather(f32[1,16,8]{1,2,0:T(8,128)S(1)} %get-tuple-element.392), channel_id=2, replica_groups=mesh['dp'=4,'ctx'=64,'mp'=2] {'ctx'}, dimensions={0}, use_global_device_ids=true | all-gather | bytes 33280 | tf_op jit(solution)/shard_map/all_gather | solution.py:21
  169.1 53.8 %all-gather.7.cloned.1.call-done = f32[1024,8,1,128]{3,1,2,0:T(8,128)} async-done(((f32[16,8,1,128]{3,1,2,0:T(8,128)}), f32[1024,8,1,128]{3,1,2,0:T(8,128)}) %all-gather.7.cloned.1.call-update) | async-done | bytes 4194320 | tf_op jit(solution)/shard_map/all_gather | solution.py:21
  223.0 8.3 multiply_reduce_fusion.2
  232.6 2.5 all-reduce.5
  235.1 3.2 fusion.85
  241.1 2.9 copy.51
  243.9 2.4 reshape.384
  246.3 2.4 reshape.382
  248.7 2.9 fusion.72
  252.8 232.8 %all-gather.9.cloned.1.call-done = f32[1024,8,128]{2,1,0:T(8,128)} async-done(((f32[16,8,128]{2,1,0:T(8,128)}), f32[1024,8,128]{2,1,0:T(8,128)}) %all-gather.9.cloned.1.call-update) | async-done | bytes 4194320 | tf_op jit(solution)/shard_map/all_gather | solution.py:21
  485.6 107.9 %while.53 = (s32[]{:T(128)}, f32[16,8,128]{2,1,0:T(8,128)S(1)}, s32[]{:T(128)}, f32[64,16,8]{1,2,0:T(8,128)}, f32[64,16,8,128]{3,2,1,0:T(8,128)}, /*index=5*/s32[]{:T(128)}, s32[]{:T(128)}, s32[]{:T(128)}, s32[]{:T(128)}) while((s32[]{:T(128)}, f32[16,8,128]{2,1,0:T(8,128)S(1)}, s32[]{:T(128)}, f32[64,16,8]{1,2,0:T(8,128)}, ...), condition=%wide.region_9.10_spmd, body=%wide.region_8.9_spmd.sunk | while | flops 32774 | bytes 199315 | solution.py:30
  594.1 146.1 %while.54 = (s32[]{:T(128)}, f32[16,8,128]{2,1,0:T(8,128)}, f32[16,8]{1,0:T(8,128)}, f32[16,128,128]{2,1,0:T(8,128)}, f32[16,128,128]{2,1,0:T(8,128)}, /*index=5...) while((s32[]{:T(128)}, f32[16,8,128]{2,1,0:T(8,128)}, ...), condition=%wide.region_15.16_spmd.clone, body=%wide.region_10.15_spmd.clone.sunk | while | flops 202687648 | bytes 3312593 | solution.py:144
  741.6 2.8 copy.59
  744.4 2.4 reshape.385
  746.8 2.9 slice_multiply_fusion.6
  751.2 3.4 fusion.54
  755.3 2.8 fusion.38
  762.0 1364.5 %all-reduce.3 = (f32[8,16]{1,0:T(8,128)}, f32[2048]{0:T(1024)}, f32[2048]{0:T(1024)}) all-reduce(f32[8,16]{1,0:T(8,128)S(1)} %bitcast_multiply_fusion.4, f32[2048]{0:T(1024)} %get-tuple-element.308, f32[2048]{0:T(1024)S(1)} %copy-done.24), channel_id=1, replica_groups=mesh['dp'=4,'ctx'=64,'mp'=2] {'dp','ctx'}, use_global_device_ids=true, to_apply=%region_24.25 | all-reduce | flops 4224 | bytes 33792 | tf_op jit(solution)/shard_map/psum | solution.py:171
  2126.5 3.5 fusion.57
  (622 shorter events, 297.0 us)
Async XLA Ops:
  7.2 215.7 %all-gather.7.cloned.1.call-start = ((), (), s32[]{:S(2)}) async-start(), calls=%async_computation | async-start | bytes 4259840 | tf_op jit(solution)/shard_map/all_gather | solution.py:21
  8.1 4.3 collective-permute-start
  11.6 9.9 copy-start.12
  12.4 9.1 copy-start.14
  63.0 10.0 copy-start.26
  63.0 10.7 copy-start.23
  73.6 411.9 %all-gather.9.cloned.1.call-start = ((), (), s32[]{:S(2)}) async-start(), calls=%async_computation.1 | async-start | bytes 4259840 | tf_op jit(solution)/shard_map/all_gather | solution.py:21
  73.8 149.1 %copy-start.21 = (f32[16,8]{1,0:T(8,128)}, f32[16,8]{1,0:T(8,128)S(1)}, u32[]{:S(2)}) copy-start(f32[16,8]{1,0:T(8,128)S(1)} %copy.49) | copy-start | bytes 1540
  73.8 94.1 %copy-start.9 = (f32[16,8,16,128]{3,1,2,0:T(8,128)S(1)}, f32[16,8,16,128]{3,1,2,0:T(8,128)}, u32[]{:S(2)}) copy-start(f32[16,8,16,128]{3,1,2,0:T(8,128)} %get-tuple-element.382) | copy-start | bytes 3145732
  167.8 55.1 %copy-start.31 = (f32[128]{0:T(128)}, f32[128]{0:T(128)S(1)}, u32[]{:S(2)}) copy-start(f32[128]{0:T(128)S(1)} %iota_add_fusion) | copy-start | bytes 1540
  222.9 8.3 copy-start.1
  222.9 8.3 copy-start.7
  222.9 8.3 copy-start.16
  222.9 8.3 copy-start.18
  231.2 1.4 copy-start.3
  231.2 3.9 copy-start.19
  232.6 6.7 copy-start.22
  232.6 6.7 copy-start.32
  235.1 13.6 copy-start.29
  235.1 16.5 copy-start.27
  241.0 1888.9 %all-reduce.8.cloned.1.call-start = ((), (), s32[]{:S(2)}) async-start(), calls=%async_computation.2 | async-start | bytes 589824 | tf_op jit(solution)/shard_map/psum | solution.py:171
  248.7 2.9 copy-start.2
  248.7 2.9 copy-start.10
  740.2 6.6 copy-start.17
  740.2 6.6 copy-start.20
  740.2 6.6 copy-start.28
  740.2 6.6 copy-start.30
  749.8 1.4 copy-start.4
  755.3 6.6 copy-start.25
  755.3 6.7 copy-start.24
  758.1 1.7 copy-start.5
  759.8 1366.6 %collective-permute-start.1 = (f32[6,3,2048]{2,0,1:T(8,128)S(1)}, f32[6,3,2048]{2,0,1:T(8,128)S(1)}, u32[]{:S(2)}, u32[]{:S(2)}) collective-permute-start(f32[6,3,2048]{2,0,1:T(8,128)S(1)} %slice.156), channel_id=1, source_target_pairs={{2,0},{4,2},{6,4},{8,6},{10,8},{12,10},{14,12},{16,14},{18,16},{20... | collective-permute-start | bytes 442376 | tf_op jit(solution)/shard_map/ppermute | solution.py:14
  (6 other events, 5.3 us)
Sparse Core Ops, SparseCore 0:
  73.8 149.0 all-gather.6
  241.1 244.3 all-gather.8
  762.1 380.4 all-reduce.7
where the time goes:
time: 2150 us; the launch traced here: 2140 us
  blocking collectives  1460 us (68%)
  waiting for transfers between devices  287 us (13%)
  local copies, waits for them, and re-layouts  156 us (7%)
  other arithmetic  156 us (7%)
  matrix products  62.4 us (3%)
    psum x1, blocking collectives, local(): lax.psum((conv_local, rate_local, residue_local, skip_local, gain_local),...  1360 us
    all_gather x2, waiting for transfers between devices, carried_in(): gathered = jax.tree.map(lambda a: lax.all_gather(a, axis), part)  287 us
    all_gather x1, blocking collectives, carried_in(): gathered = jax.tree.map(lambda a: lax.all_gather(a, axis), part)  91.5 us
    add x63, other arithmetic, compose_back(): return (earlier[0] * later[0], earlier[1] * later[0][..., None] + later[1])  58.2 us
    mul x126, local copies, waits for them, and re-layouts, compose_back(): return (earlier[0] * later[0], earlier[1] * later[0][..., None] + later[1])  47.7 us
  transfers between devices with their start and end apart: 5, of which 2 were waited for; matrix products, arithmetic and copies ran while one was open for 1% of the time, Pallas kernels for 0%

commit v1 on v0

--- a/solution.py
+++ b/solution.py
@@ -168,9 +168,8 @@
         [jnp.zeros((length - halo_rows, 3, channels), jnp.float32), incoming], axis=0
     )
     feature_grad = dlocal.astype(jnp.bfloat16)[None]
-    totals = lax.psum(
-        (conv_local, rate_local, residue_local, skip_local, gain_local), ("dp", "ctx")
-    )
+    partial = lax.psum((conv_local, rate_local, residue_local, skip_local, gain_local), "ctx")
+    totals = lax.psum(partial, "dp")
     return (block_out[None], feature_grad, totals[0], totals[1], totals[2], totals[3], totals[4])
 
 

time: 2150 us -> 1100 us (0.51)
  blocking collectives: 1460 us -> 389 us
  waiting for transfers between devices: 287 us -> 327 us
    psum x1, blocking collectives: 1360 us -> 277 us  [local(): lax.psum((conv_local, rate_local, residue_local, skip_local, gain_local),...]
    psum x0 -> x1, waiting for transfers between devices: none -> 41.1 us  [local(): totals = lax.psum(partial, 'dp')]
  transfers between devices with their start and end apart: 5 -> 6, of which waited for: 2 -> 3; matrix products, arithmetic and copies ran while one was open for 1% -> 3% of each run, Pallas kernels for 0% -> 0%
where the time goes in v1:
time: 1100 us; the launch traced here: 1090 us
  blocking collectives  389 us (35%)
  waiting for transfers between devices  327 us (30%)
  other arithmetic  154 us (14%)
  local copies, waits for them, and re-layouts  136 us (12%)
  matrix products  62.4 us (6%)
  between operations  14.1 us (1%)
    all_gather x2, waiting for transfers between devices, carried_in(): gathered = jax.tree.map(lambda a: lax.all_gather(a, axis), part)  286 us
    psum x1, blocking collectives, local(): lax.psum((conv_local, rate_local, residue_local, skip_local, gain_local),...  277 us
    all_gather x1, blocking collectives, carried_in(): gathered = jax.tree.map(lambda a: lax.all_gather(a, axis), part)  92.1 us
    add x63, other arithmetic, compose_back(): return (earlier[0] * later[0], earlier[1] * later[0][..., None] + later[1])  58.2 us
    mul x126, local copies, waits for them, and re-layouts, compose_back(): return (earlier[0] * later[0], earlier[1] * later[0][..., None] + later[1])  47.7 us
    psum x1, waiting for transfers between devices, local(): totals = lax.psum(partial, 'dp')  41.1 us
    dot_general x16, matrix products, forward_plain(): return jnp.einsum('pts,sc->ptc', matrix, product_block, precision=HIGHEST)  36.8 us
    dynamic_update_slice x48, local copies, waits for them, and re-layouts, local(): lax.map(backward_adjoint, (rate_rows, grouped, dgrouped, states, weights,...  30.8 us
  transfers between devices with their start and end apart: 6, of which 3 were waited for; matrix products, arithmetic and copies ran while one was open for 3% of the time, Pallas kernels for 0%

profile of v1, /device:TPU:0, one launch (start us, length us, event | category | flops | bytes accessed | tf_op | source)
XLA Modules:
  0.0 1086.8 jit_solution(8587781748722761232)
XLA Ops:
  12.3 7.5 fusion.48
  25.1 38.0 %while.51 = (s32[]{:T(128)}, f32[16,8,128,128]{3,2,1,0:T(8,128)}, f32[16,8]{1,0:T(8,128)S(1)}, f32[16,128,128]{2,1,0:T(8,128)}, s32[]{:T(128)}) while((s32[]{:T(128)}, f32[16,8,128,128]{3,2,1,0:T(8,128)}, f32[16,8]{1,0:T(8,128)S(1)}, f32[16,128,128]{2,1,0:T(8,128)}, s32[]{:T(128)}) %tuple.146), condition=%wide.region_1.2_spmd, body=%wide.region_0.1_spmd.sunk | while | flops 201654288 | bytes 754849 | solution.py:76
  25.2 2.3 fusion.110
  27.6 2.4 fusion.110
  34.8 2.3 fusion.110
  44.3 2.3 fusion.110
  46.7 2.3 fusion.110
  53.8 2.3 fusion.110
  63.2 9.9 copy.50
  76.4 92.1 %all-gather.3 = f32[64,16,8]{1,2,0:T(8,128)} all-gather(f32[1,16,8]{1,2,0:T(8,128)S(1)} %get-tuple-element.397), channel_id=2, replica_groups=mesh['dp'=4,'ctx'=64,'mp'=2] {'ctx'}, dimensions={0}, use_global_device_ids=true | all-gather | bytes 33280 | tf_op jit(solution)/shard_map/all_gather | solution.py:21
  169.7 53.5 %all-gather.7.cloned.1.call-done = f32[1024,8,1,128]{3,1,2,0:T(8,128)} async-done(((f32[16,8,1,128]{3,1,2,0:T(8,128)}), f32[1024,8,1,128]{3,1,2,0:T(8,128)}) %all-gather.7.cloned.1.call-update) | async-done | bytes 4194320 | tf_op jit(solution)/shard_map/all_gather | solution.py:21
  223.3 9.2 multiply_reduce_fusion.2
  232.5 2.9 fusion.67
  235.4 2.4 all-reduce.7
  237.8 3.2 fusion.85
  243.8 2.9 copy.51
  246.7 2.4 reshape.384
  249.0 2.4 reshape.382
  251.4 2.8 fusion.72
  254.2 2.4 fusion.81
  256.6 232.0 %all-gather.9.cloned.1.call-done = f32[1024,8,128]{2,1,0:T(8,128)} async-done(((f32[16,8,128]{2,1,0:T(8,128)}), f32[1024,8,128]{2,1,0:T(8,128)}) %all-gather.9.cloned.1.call-update) | async-done | bytes 4194320 | tf_op jit(solution)/shard_map/all_gather | solution.py:21
  488.6 107.7 %while.53 = (s32[]{:T(128)}, f32[16,8,128]{2,1,0:T(8,128)S(1)}, s32[]{:T(128)}, f32[64,16,8]{1,2,0:T(8,128)}, f32[64,16,8,128]{3,2,1,0:T(8,128)}, /*index=5*/s32[]{:T(128)}, s32[]{:T(128)}, s32[]{:T(128)}, s32[]{:T(128)}) while((s32[]{:T(128)}, f32[16,8,128]{2,1,0:T(8,128)S(1)}, s32[]{:T(128)}, f32[64,16,8]{1,2,0:T(8,128)}, ...), condition=%wide.region_9.10_spmd, body=%wide.region_8.9_spmd.sunk | while | flops 32774 | bytes 199315 | solution.py:30
  596.3 114.5 %while.54 = (s32[]{:T(128)}, f32[16,8,128]{2,1,0:T(8,128)S(1)}, f32[16,8]{1,0:T(8,128)}, f32[16,128,128]{2,1,0:T(8,128)}, f32[16,128,128]{2,1,0:T(8,128)}, /*ind...) while((s32[]{:T(128)}, f32[16,8,128]{2,1,0:T(8,128)S(1)}, ...), condition=%wide.region_15.16_spmd.clone, body=%wide.region_10.15_spmd.clone.sunk | while | flops 202687648 | bytes 3312085 | solution.py:144
  710.8 2.8 copy.59
  713.7 2.4 reshape.385
  716.0 2.7 slice_multiply_fusion.6
  720.9 3.4 fusion.54
  729.4 5.9 fusion.38
  738.3 276.7 %all-reduce.3 = (f32[8,16]{1,0:T(8,128)S(1)}, f32[2048]{0:T(1024)S(1)}, f32[2048]{0:T(1024)S(1)}) all-reduce(f32[8,16]{1,0:T(8,128)S(1)} %bitcast_multiply_fusion.4, f32[2048]{0:T(1024)} %get-tuple-element.308, f32[2048]{0:T(1024)S(1)} %get-tuple-element.307), channel_id=1, replica_groups=mesh['dp'=4,'ctx'=64,'mp'=2] {'ctx'}, use_global_device_ids=true, to_apply=%region_25.26 | all-reduce | flops 4224 | bytes 33792 | tf_op jit(solution)/shard_map/psum | solution.py:171
  1015.0 17.5 %all-reduce.5 = (f32[8,16]{1,0:T(8,128)}, f32[2048]{0:T(1024)}, f32[2048]{0:T(1024)}) all-reduce(f32[8,16]{1,0:T(8,128)S(1)} %get-tuple-element.359, f32[2048]{0:T(1024)S(1)} %get-tuple-element.360, f32[2048]{0:T(1024)S(1)} %get-tuple-element.361), channel_id=1, replica_groups=mesh['dp'=4,'ctx'=64,'mp'=2] {'dp'}, use_global_device_ids=true, to_apply=%region_26.27 | all-reduce | flops 4224 | bytes 33792 | tf_op jit(solution)/shard_map/psum | solution.py:172
  1032.5 3.5 fusion.57
  1036.0 41.1 %all-reduce.13.cloned.1.call-done = (f32[7,3,2048]{2,1,0:T(4,128)}, f32[8,2048]{1,0:T(8,128)}) async-done(((f32[7,3,2048]{2,1,0:T(4,128)}, f32[8,2048]{1,0:T(8,128)}), (f32[7,3,2048]{2,1,0:T(4,128)}, f32[8,2048]{1,0:T(8,128)})) %all-reduce.13.cloned.1.call-update) | async-done | bytes 237584 | tf_op jit(solution)/shard_map/psum | solution.py:172
  (602 shorter events, 274.6 us)
Async XLA Ops:
  7.2 216.1 %all-gather.7.cloned.1.call-start = ((), (), s32[]{:S(2)}) async-start(), calls=%async_computation | async-start | bytes 4259840 | tf_op jit(solution)/shard_map/all_gather | solution.py:21
  8.1 4.2 collective-permute-start
  11.3 10.0 copy-start.6
  11.3 10.0 copy-start.7
  11.4 9.9 copy-start.8
  11.4 9.9 copy-start.9
  11.4 9.9 copy-start.10
  11.5 9.9 copy-start.11
  12.2 9.2 copy-start.12
  22.8 1.0 copy-start.1
  63.2 10.0 copy-start.18
  63.2 10.7 copy-start.17
  73.8 414.8 %all-gather.9.cloned.1.call-start = ((), (), s32[]{:S(2)}) async-start(), calls=%async_computation.1 | async-start | bytes 4259840 | tf_op jit(solution)/shard_map/all_gather | solution.py:21
  73.9 94.6 %copy-start.4 = (f32[16,8,16,128]{3,1,2,0:T(8,128)S(1)}, f32[16,8,16,128]{3,1,2,0:T(8,128)}, u32[]{:S(2)}) copy-start(f32[16,8,16,128]{3,1,2,0:T(8,128)} %get-tuple-element.387) | copy-start | bytes 3145732
  75.2 148.1 %copy-start.15 = (f32[8,2048]{1,0:T(8,128)S(1)}, f32[8,2048]{1,0:T(8,128)}, u32[]{:S(2)}) copy-start(f32[8,2048]{1,0:T(8,128)} %param.18) | copy-start | bytes 196612
  223.3 9.2 copy-start.2
  223.3 9.2 copy-start.14
  223.3 9.2 copy-start.16
  237.8 13.6 %copy-start.19 = (f32[128]{0:T(128)}, f32[128]{0:T(128)S(1)}, u32[]{:S(2)}) copy-start(f32[128]{0:T(128)S(1)} %get-tuple-element.398) | copy-start | bytes 1540
  241.0 1.1 copy-start.3
  243.7 788.8 %all-reduce.11.cloned.1.call-start = ((), (), s32[]{:S(2)}) async-start(), calls=%async_computation.2 | async-start | bytes 589824 | tf_op jit(solution)/shard_map/psum | solution.py:171
  251.4 2.9 copy-start.5
  710.8 7.9 copy-start.13
  710.8 5.2 copy-start.20
  718.8 2.0 copy-start
  729.1 348.0 %all-reduce.13.cloned.1.call-start = ((), (), s32[]{:S(2)}) async-start(), calls=%async_computation.3 | async-start | bytes 589824 | tf_op jit(solution)/shard_map/psum | solution.py:172
  737.0 295.5 %collective-permute-start.1 = (f32[6,3,2048]{2,0,1:T(8,128)S(1)}, f32[6,3,2048]{2,0,1:T(8,128)S(1)}, u32[]{:S(2)}, u32[]{:S(2)}) collective-permute-start(f32[6,3,2048]{2,0,1:T(8,128)S(1)} %slice.156), channel_id=1, source_target_pairs={{2,0},{4,2},{6,4},{8,6},{10,8},{12,10},{14,12},{16,14},{18,16},{20... | collective-permute-start | bytes 442376 | tf_op jit(solution)/shard_map/ppermute | solution.py:14
Sparse Core Ops, SparseCore 0:
  73.9 149.2 all-gather.6
  243.9 244.6 all-gather.8
  729.2 251.4 all-reduce.10
  1032.6 44.4 all-reduce.12
